TPU v7x, 256 devices: a whole 4x4x8 slice. The times are simulated.
256 devices in a mesh: rows: 128 (over y_lo, z, x, core), sub: 2 (over y_hi).
Axes of the slice: x: 4, y: 4 (y_hi: 2, y_lo: 2; y = y_hi * 2 + y_lo), z: 8, core: 2. Of those that a mesh axis runs over, the one named last changes fastest.
Arguments:
- features: bfloat16 [440, 1048576], P(None, ('rows', 'sub')), may hold values from -6 to 6
- residual: float32 [147, 1048576], P(None, ('rows', 'sub')), may hold values from -6 to 6
- coeffs: float32 [147, 1048576], P(None, ('rows', 'sub')), may hold values from -6 to 6
- inverse: float32 [2, 512, 512], replicated, may hold values from -0.25 to 0.25
- owner: int32 [2], replicated, may hold values from 0 to 255
- offsets: int32 [2, 512], replicated, may hold values from 0 to 4095, as said below
Outputs:
- new_residual: float32 [147, 1048576], P(None, ('rows', 'sub'))
- new_coeffs: float32 [147, 1048576], P(None, ('rows', 'sub'))
Inputs may be any that keep to these rules, and one draw needn't show every extreme that they name: Within one step the 512 offsets are distinct; each step holds both 0 and 4095.
All inputs are finite; a program needn't handle non-finite values.
Results may differ from a plain program's by a relative error of at most 0.0038.
Values may be sent and summed in bfloat16 or wider, within the bound.
No kernel may reach another device: no remote copies, remote signals or barrier semaphores. Data moves between devices by JAX's collectives and lax.ppermute only.
A program may use at most 128 MiB of HBM per device.

v0:
```python
import jax
import jax.numpy as jnp
from jax import lax
from jax.sharding import PartitionSpec as P

STEPS = 2


def spread(block, axis, holder):
    block = jnp.where(lax.axis_index(axis) == holder, block, jnp.zeros_like(block))
    return lax.psum(block, axis)


def kernel_rows(rows_feat, block):
    dots = jnp.dot(rows_feat.T, block, preferred_element_type=jnp.float32)
    rows_sq = jnp.sum(rows_feat.astype(jnp.float32) ** 2, axis=0)
    block_sq = jnp.sum(block.astype(jnp.float32) ** 2, axis=0)
    dist = rows_sq[:, None] + block_sq[None, :] - 2.0 * dots
    return jnp.exp(-2.0 * dist / rows_feat.shape[0]).astype(jnp.bfloat16)


def shards(features, residual, coeffs, inverse, owner, offsets):
    myself = lax.axis_index(("rows", "sub"))
    for step in range(STEPS):
        local_cols = offsets[step]
        block_res = jnp.take(residual, local_cols, axis=1)
        delta = jnp.dot(block_res, inverse[step], precision=lax.Precision.HIGHEST).astype(
            jnp.bfloat16
        )
        local_block = jnp.take(features, local_cols, axis=1)
        block, delta = (
            spread(local_block, ("rows", "sub"), owner[step]),
            spread(delta, ("rows", "sub"), owner[step]),
        )
        kernel = kernel_rows(features, block)
        update = lax.dot_general(
            delta, kernel, (((1,), (1,)), ((), ())), preferred_element_type=jnp.float32
        )
        is_owner = owner[step] == myself
        delta_wide = delta.astype(jnp.float32)
        residual = residual - update
        residual = residual.at[:, local_cols].add(jnp.where(is_owner, -0.5 * delta_wide, 0.0))
        coeffs = coeffs.at[:, local_cols].add(jnp.where(is_owner, delta_wide, 0.0))
    return (residual, coeffs)


def solution(mesh):
    return jax.shard_map(
        shards,
        mesh=mesh,
        in_specs=(
            P(None, ("rows", "sub")),
            P(None, ("rows", "sub")),
            P(None, ("rows", "sub")),
            P(),
            P(),
            P(),
        ),
        out_specs=(P(None, ("rows", "sub")), P(None, ("rows", "sub"))),
        check_vma=False,
    )
```

profile of v0, /device:TPU:1, one launch (start us, length us, event | category | flops | bytes accessed | tf_op | source)
XLA Modules:
  0.0 612.1 jit_solution(14545046482279106827)
XLA Ops:
  8.0 4.8 copy.21
  13.5 6.4 %copy.22 = bf16[440,4096]{0,1:T(8,128)(2,1)} copy(bf16[440,4096]{1,0:T(8,128)(2,1)} %param.10) | data formatting | bytes 7208960 | tf_op args[0]
  19.9 3.9 gather_fusion
  23.8 4.7 gather_fusion.1
  30.1 1.9 fusion.6
  33.6 4.9 gather_fusion.3
  39.4 2.8 multiply_reduce_fusion
  42.1 246.1 %all-reduce.7.cloned.1.call-done = (bf16[147,512]{1,0:T(8,128)(2,1)}, bf16[440,512]{0,1:T(8,128)(2,1)}) async-done(((bf16[147,512]{1,0:T(8,128)(2,1)}, bf16[440,512]{0,1:T(8,128)(2,1)}), (bf16[147,512]{1,0:T(8,128)(2,1)}, bf16[440,512]{0,1:T(8,128)(2,1)})) %all-reduce.7.cloned.1.call-update) | async-done | bytes 601104 | tf_op jit(solution)/shard_map/psum | solution.py:11
  288.2 1.2 multiply_reduce_fusion.2
  289.4 7.5 %convolution_subtract_fusion.1 = f32[147,4096]{1,0:T(8,128)} fusion(f32[147,4096]{1,0:T(8,128)S(1)} %copy-done, bf16[147,512]{1,0:T(8,128)(2,1)} %get-tuple-element.10, bf16[440,512]{0,1:T(8,128)(2,1)} %get-tuple-element.11, bf16[440,4096]{1,0:T(8,128)(2,1)} %param.10, f32[512]{0:T(512)S(1)} %multiply_reduce_fusion.2, f32[4096]{0:T(1024)S(1)} %multiply_reduce_fusion), kind=kOutput, calls=%fused_computation.18 | convolution fusion | flops 2473144320 | bytes 9040896 | tf_op jit(solution)/shard_map/dot_general | solution.py:36
  296.9 4.8 copy.23
  302.1 7.3 %scatter_fusion = f32[147,4096]{0,1:T(8,128)} fusion(f32[147,4096]{0,1:T(8,128)} %copy.23, s32[512]{0:T(512)S(1)} %bitcast.62, f32[512,147]{1,0:T(8,128)S(1)} %copy.24), kind=kCustom, calls=%fused_computation.4 | custom fusion | flops 75264 | bytes 905216 | tf_op jit(solution)/shard_map/scatter-add | solution.py:42
  309.4 3.8 gather_fusion.2
  313.1 3.1 fusion.7
  317.0 3.3 copy.29
  320.3 3.7 copy.26
  324.2 7.1 %scatter_fusion.2 = f32[147,4096]{0,1:T(8,128)} fusion(f32[147,4096]{0,1:T(8,128)} %copy.29, s32[512]{0:T(512)S(1)} %bitcast.63, f32[512,147]{1,0:T(8,128)S(1)} %copy.30), kind=kCustom, calls=%fused_computation.6 | custom fusion | flops 75264 | bytes 905216 | tf_op jit(solution)/shard_map/scatter-add | solution.py:43
  331.3 235.6 %all-reduce.5.cloned.1.call-done = (bf16[147,512]{1,0:T(8,128)(2,1)}, bf16[440,512]{0,1:T(8,128)(2,1)}) async-done(((bf16[147,512]{1,0:T(8,128)(2,1)}, bf16[440,512]{0,1:T(8,128)(2,1)}), (bf16[147,512]{1,0:T(8,128)(2,1)}, bf16[440,512]{0,1:T(8,128)(2,1)})) %all-reduce.5.cloned.1.call-update) | async-done | bytes 601104 | tf_op jit(solution)/shard_map/psum | solution.py:11
  568.1 7.5 %convolution_subtract_fusion = f32[147,4096]{1,0:T(8,128)} fusion(f32[147,4096]{1,0:T(8,128)S(1)} %copy.26, bf16[147,512]{1,0:T(8,128)(2,1)} %get-tuple-element.8, bf16[440,512]{0,1:T(8,128)(2,1)} %get-tuple-element.9, bf16[440,4096]{1,0:T(8,128)(2,1)} %param.10, f32[512]{0:T(512)S(1)} %multiply_reduce_fusion.1, f32[4096]{0:T(1024)S(1)} %multiply_reduce_fusion), kind=kOutput, calls=%fused_computation.17 | convolution fusion | flops 2473144320 | bytes 9040896 | tf_op jit(solution)/shard_map/dot_general | solution.py:36
  575.6 4.8 copy.27
  580.8 7.2 %scatter_fusion.1 = f32[147,4096]{0,1:T(8,128)} fusion(f32[147,4096]{0,1:T(8,128)} %copy.27, s32[512]{0:T(512)S(1)} %bitcast.60, f32[512,147]{1,0:T(8,128)S(1)} %copy.28), kind=kCustom, calls=%fused_computation.5 | custom fusion | flops 75264 | bytes 905216 | tf_op jit(solution)/shard_map/scatter-add | solution.py:42
  587.9 5.0 copy.32
  593.1 7.1 %scatter_fusion.3 = f32[147,4096]{0,1:T(8,128)} fusion(f32[147,4096]{0,1:T(8,128)} %scatter_fusion.2, s32[512]{0:T(512)S(1)} %bitcast.61, f32[512,147]{1,0:T(8,128)S(1)} %copy.31), kind=kCustom, calls=%fused_computation.7 | custom fusion | flops 75264 | bytes 905216 | tf_op jit(solution)/shard_map/scatter-add | solution.py:43
  600.2 5.0 copy.33
  (36 shorter events, 5.6 us)
Async XLA Ops:
  7.2 5.7 copy-start.6
  7.2 281.0 %all-reduce.7.cloned.1.call-start = ((), (), s32[]{:S(2)}) async-start(), calls=%async_computation.1 | async-start | bytes 1359872 | tf_op jit(solution)/shard_map/psum | solution.py:11
  19.9 10.2 %copy-start.2 = (f32[2,512,512]{2,1,0:T(8,128)S(1)}, f32[2,512,512]{2,1,0:T(8,128)}, u32[]{:S(2)}) copy-start(f32[2,512,512]{2,1,0:T(8,128)} %param.13) | copy-start | bytes 6291460
  23.8 8.3 %copy-start.5 = (s32[2,512]{1,0:T(2,128)S(1)}, s32[2,512]{1,0:T(2,128)}, u32[]{:S(2)}) copy-start(s32[2,512]{1,0:T(2,128)} %param.15) | copy-start | bytes 12292
  32.1 534.8 %all-reduce.5.cloned.1.call-start = ((), (), s32[]{:S(2)}) async-start(), calls=%async_computation | async-start | bytes 1359872 | tf_op jit(solution)/shard_map/psum | solution.py:11
  33.5 255.9 %copy-start = (f32[147,4096]{1,0:T(8,128)S(1)}, f32[147,4096]{1,0:T(8,128)}, u32[]{:S(2)}) copy-start(f32[147,4096]{1,0:T(8,128)} %param.11) | copy-start | bytes 7225348
  296.9 4.9 copy-start.3
  302.1 14.9 %copy-start.1 = (f32[147,4096]{1,0:T(8,128)S(1)}, f32[147,4096]{1,0:T(8,128)}, u32[]{:S(2)}) copy-start(f32[147,4096]{1,0:T(8,128)} %param.12) | copy-start | bytes 7225348
  575.6 4.9 copy-start.4
Sparse Core Ops, SparseCore 0:
  32.2 255.9 all-reduce.6
  316.4 250.4 all-reduce.4
where the time goes:
time: 613 us; the launch traced here: 612 us
  waiting for transfers between devices  482 us (79%)
  local copies, waits for them, and re-layouts  57.3 us (9%)
  other arithmetic  36 us (6%)
  matrix products  20 us (3%)
  between operations  16.9 us (3%)
    psum x2, waiting for transfers between devices, spread(): return lax.psum(block, axis)  482 us
    unnamed x19, local copies, waits for them, and re-layouts  24.5 us
    dot_general x2, matrix products, shards(): lax.dot_general(delta, kernel, (((1,), (1,)), ((), ())), preferred_elemen...  15 us
    scatter-add x2, other arithmetic, shards(): residual.at[:, local_cols].add(jnp.where(is_owner, -0.5 * delta_wide, 0.0))  14.5 us
    scatter-add x2, other arithmetic, shards(): coeffs = coeffs.at[:, local_cols].add(jnp.where(is_owner, delta_wide, 0.0))  14.2 us
  transfers between devices with their start and end apart: 2, of which 2 were waited for; matrix products, arithmetic and copies ran while one was open for 4% of the time, Pallas kernels for 0%

commit v1 on v0

v1 whole, which is shorter than its diff:
```python
import math

import jax
import jax.numpy as jnp
from jax import lax
from jax.experimental import pallas as pl
from jax.experimental.pallas import tpu as pltpu
from jax.sharding import Mesh, PartitionSpec as P

STEPS = 2
F, C, B, R = 440, 147, 512, 4096
FP, CP = 448, 160
ROWS = 768
HALF = 256
GROUPS = 32
PIECE = 48
KT = 512
TILE = 512
AXES = ("yl", "zh", "zl", "x", "c", "yh")
SPREAD = ("yl", "zl", "x", "yh")
BF, F32 = jnp.bfloat16, jnp.float32
HIGH = lax.Precision.HIGHEST


def split(value, terms):
    parts = []
    for _ in range(terms):
        part = value.astype(BF)
        parts.append(part)
        value = value - part.astype(F32)
    return parts


def dot(a, b):
    return jnp.dot(a, b, preferred_element_type=F32)


def pick_kernel(info, feat, res, inv, offs, own, sib, left, acc, msg):
    tile = pl.program_id(0)
    last = pl.num_programs(0) - 1
    for step in range(STEPS):

        @pl.when(info[step] == 1)
        def _():
            left[:F, :] = feat[...]
            for i, part in enumerate(split(res[...], 3)):
                left[FP + i * CP : FP + i * CP + C, :] = part
            row = lax.broadcasted_iota(jnp.int32, (KT, B), 0) + tile * KT
            hot = jnp.where(row == offs[step : step + 1, :], 1.0, 0.0).astype(BF)
            found = dot(left[...], hot)

            @pl.when(tile == 0)
            def _():
                acc[step] = found

            @pl.when(tile > 0)
            def _():
                acc[step] += found

        @pl.when((info[step] == 1) & (tile == last))
        def _():
            msg[:FP, :] = acc[step, :FP, :].astype(BF)
            cols = acc[step, FP : FP + C, :] + (
                acc[step, FP + CP : FP + CP + C, :] + acc[step, FP + 2 * CP : FP + 2 * CP + C, :]
            )
            prod = jnp.dot(cols, inv[step], precision=HIGH, preferred_element_type=F32)
            parts = split(prod, 2)
            msg[FP : FP + C, :] = parts[0]
            if step == 1:
                msg[FP + CP : FP + CP + C, :] = parts[1]
            mine = info[2]
            for out, half in ((own, mine), (sib, 1 - mine)):
                for cb in range(2):
                    lanes = pl.ds(pl.multiple_of(half * HALF + cb * 128, 128), 128)
                    for rg in range(16):
                        out[cb * 16 + rg, PIECE * step : PIECE * (step + 1), :] = msg[
                            rg * PIECE : (rg + 1) * PIECE, lanes
                        ]


def pick(info, features, residual, inverse, offsets):
    whole = lambda *shape: pl.BlockSpec(shape, lambda i, info: (0,) * len(shape))
    piece = jax.ShapeDtypeStruct((GROUPS, 2 * PIECE, 128), BF)
    return pl.pallas_call(
        pick_kernel,
        grid_spec=pltpu.PrefetchScalarGridSpec(
            num_scalar_prefetch=1,
            grid=(R // KT,),
            in_specs=[
                pl.BlockSpec((F, KT), lambda i, info: (0, i)),
                pl.BlockSpec((C, KT), lambda i, info: (0, i)),
                whole(STEPS, B, B),
                whole(STEPS, B),
            ],
            out_specs=[whole(GROUPS, 2 * PIECE, 128)] * 2,
            scratch_shapes=[
                pltpu.VMEM((FP + 3 * CP, KT), BF),
                pltpu.VMEM((STEPS, FP + 3 * CP, B), F32),
                pltpu.VMEM((ROWS, B), BF),
            ],
        ),
        out_shape=[piece, piece],
        compiler_params=pltpu.CompilerParams(vmem_limit_bytes=48 * 1024 * 1024),
        name="pick",
    )(info, features, residual, inverse, offsets)


def update_kernel(
    info, own, sib, feat, res, coef, inv, offs, offs_col, new_res, new_coef, blk, right, blkt, delta
):
    scale = 4.0 * math.log2(math.e) / F
    mine = info[2]

    def kernel_of(lhs, rhs):
        return jnp.exp2(dot(lhs, rhs) * scale).astype(BF)

    @pl.when(pl.program_id(0) == 0)
    def _():
        for src, half in ((own, mine), (sib, 1 - mine)):
            for cb in range(2):
                lanes = pl.ds(pl.multiple_of(half * HALF + cb * 128, 128), 128)
                for rg in range(16):
                    for step in range(STEPS):
                        blk[step, rg * PIECE : (rg + 1) * PIECE, lanes] = src[
                            cb * 16 + rg, PIECE * step : PIECE * (step + 1), :
                        ]
        ones = jnp.ones((3, B), BF)
        for step in range(STEPS):
            wide = blk[step, :F, :].astype(F32)
            norm = split(-0.5 * jnp.sum(wide * wide, axis=0, keepdims=True), 3)
            zero = jnp.zeros((2, B), F32)
            tail = [part.astype(F32) for part in norm] + [jnp.ones((3, B), F32), zero]
            full = jnp.concatenate([wide] + tail, axis=0)
            blkt[step * B : (step + 1) * B, :] = full.T.astype(BF)
            if step == 1:
                tail = [jnp.ones((3, B), F32)] + [part.astype(F32) for part in norm] + [zero]
                right[:, :B] = jnp.concatenate([wide] + tail, axis=0).astype(BF)
        first = blk[0, FP : FP + C, :]
        delta[:, :B] = first
        change = dot(first, kernel_of(blkt[:B, :], right[:, :B]))
        same = (offs_col[:, 0:1] == offs[1:2, :]) & (info[3] == 1)
        change = change + dot(first, jnp.where(same, 0.5, 0.0).astype(BF))
        base = blk[1, FP : FP + C, :].astype(F32) + blk[1, FP + CP : FP + CP + C, :].astype(F32)
        after = base - jnp.dot(change, inv[1], precision=HIGH, preferred_element_type=F32)
        delta[:, B:] = after.astype(BF)

    right[:F, :] = feat[...]
    wide = feat[...].astype(F32)
    norm = split(-0.5 * jnp.sum(wide * wide, axis=0, keepdims=True), 3)
    tail = [jnp.ones((3, TILE), F32)] + [part.astype(F32) for part in norm]
    right[F:, :] = jnp.concatenate(tail + [jnp.zeros((2, TILE), F32)], axis=0).astype(BF)
    left = delta[...]
    new_res[...] = res[...] - dot(left, kernel_of(blkt[...], right[...]))
    new_coef[...] = coef[...]
    for step in range(STEPS):

        @pl.when(info[step] == 1)
        def _():
            col = lax.broadcasted_iota(jnp.int32, (B, TILE), 1) + pl.program_id(0) * TILE
            hot = jnp.where(col == offs_col[:, step : step + 1], 1.0, 0.0).astype(BF)
            placed = dot(delta[:, step * B : (step + 1) * B], hot)
            new_res[...] -= 0.5 * placed
            new_coef[...] += placed


def update(info, own, sib, features, residual, coeffs, inverse, offsets):
    whole = lambda *shape: pl.BlockSpec(shape, lambda i, info: (0,) * len(shape))
    tiles = lambda rows: pl.BlockSpec((rows, TILE), lambda i, info: (0, i))
    out = jax.ShapeDtypeStruct((C, R), F32)
    return pl.pallas_call(
        update_kernel,
        grid_spec=pltpu.PrefetchScalarGridSpec(
            num_scalar_prefetch=1,
            grid=(R // TILE,),
            in_specs=[
                whole(GROUPS, 2 * PIECE, 128),
                whole(GROUPS, 2 * PIECE, 128),
                tiles(F),
                tiles(C),
                tiles(C),
                whole(STEPS, B, B),
                whole(STEPS, B),
                whole(B, STEPS),
            ],
            out_specs=[tiles(C), tiles(C)],
            scratch_shapes=[
                pltpu.VMEM((STEPS, ROWS, B), BF),
                pltpu.VMEM((FP, TILE), BF),
                pltpu.VMEM((STEPS * B, FP), BF),
                pltpu.VMEM((C, STEPS * B), BF),
            ],
        ),
        out_shape=[out, out],
        compiler_params=pltpu.CompilerParams(vmem_limit_bytes=48 * 1024 * 1024),
        name="update",
    )(info, own, sib, features, residual, coeffs, inverse, offsets, offsets.T)


def chosen(stack, first, second):
    return jnp.concatenate(
        [
            lax.dynamic_index_in_dim(stack, first, 0, False)[:PIECE],
            lax.dynamic_index_in_dim(stack, second, 0, False)[PIECE:],
        ],
        axis=0,
    )


def exchange(piece, axes, count):
    copies = jnp.broadcast_to(piece[None], (count,) + piece.shape)
    return lax.all_to_all(copies, axes, 0, 0, tiled=True)


def shards(features, residual, coeffs, inverse, owner, offsets):
    me = lax.axis_index(AXES)
    core = lax.axis_index("c")
    same = (owner[0] == owner[1]).astype(jnp.int32)
    holds = (owner == me).astype(jnp.int32)
    info = jnp.stack([holds[0], holds[1], core, same])
    o_yh, o_c, o_x = owner % 2, owner // 2 % 2, owner // 4 % 4
    o_zl, o_zh, o_yl = owner // 16 % 2, owner // 32 % 4, owner // 128
    group = ((o_yl * 2 + o_zl) * 4 + o_x) * 2 + o_yh

    own, sib = pick(info, features, residual, inverse, offsets)
    got = lax.ppermute(sib, "c", [(0, 1), (1, 0)])
    rows = lax.broadcasted_iota(jnp.int32, own.shape, 1)
    here = jnp.where(rows < PIECE, o_c[0], o_c[1]) == core
    half = jnp.where(here, own, got)
    part = chosen(lax.all_to_all(half, SPREAD, 0, 0, tiled=True), group[0], group[1])
    part = chosen(exchange(part, "zh", 4), o_zh[0], o_zh[1])
    own = exchange(part, SPREAD, GROUPS)
    sib = lax.ppermute(own, "c", [(0, 1), (1, 0)])
    return update(info, own, sib, features, residual, coeffs, inverse, offsets)


def solution(mesh):
    fine = Mesh(mesh.devices.reshape(2, 4, 2, 4, 2, 2), AXES)
    cols = P(None, AXES)
    return jax.shard_map(
        shards,
        mesh=fine,
        in_specs=(cols, cols, cols, P(), P(), P()),
        out_specs=(cols, cols),
        check_vma=False,
    )
```

time: 613 us -> 92.8 us (0.15)
  waiting for transfers between devices: 482 us -> 14.8 us
  local copies, waits for them, and re-layouts: 57.3 us -> 7.47 us
  other arithmetic: 36 us -> 3.09 us
  starting transfers between devices: 0.08 us -> 23.5 us
  matrix products: 20 us -> 0 us
  Pallas kernels: 0 us -> 18.5 us
  blocking collectives: 0 us -> 14.9 us
  between operations: 16.9 us -> 9.75 us
    psum x2 -> x0, waiting for transfers between devices: 482 us -> none  [spread(): return lax.psum(block, axis)]
    scatter-add x4 -> x0, other arithmetic: 28.7 us -> none  [the longest x2 14.5 us: shards(): residual.at[:, local_cols].add(jnp.where(is_owner, -0.5 * delta_wide, 0.0))]
    unnamed x19 -> x13, local copies, waits for them, and re-layouts: 24.5 us -> 4.14 us
    dot_general x4 -> x0, matrix products: 20 us -> none  [the longest x2 15 us: shards(): lax.dot_general(delta, kernel, (((1,), (1,)), ((), ())), preferred_elemen...]
    pallas_call x0 -> x2, Pallas kernels: none -> 18.5 us  [the longest x1 13.6 us: update(): pl.pallas_call(update_kernel, grid_spec=pltpu.PrefetchScalarGridSpec(num_...]
    gather x4 -> x0, local copies, waits for them, and re-layouts: 17.2 us -> none  [the longest x2 9.58 us: shards(): local_block = jnp.take(features, local_cols, axis=1)]
    all_to_all x0 -> x2, starting transfers between devices: none -> 15.9 us  [the longest x1 10.3 us: shards(): lax.all_to_all(half, SPREAD, 0, 0, tiled=True)]
    all_to_all x0 -> x1, blocking collectives: none -> 14.9 us  [exchange(): return lax.all_to_all(copies, axes, 0, 0, tiled=True)]
  transfers between devices with their start and end apart: 2 -> 4, of which waited for: 2 -> 3; matrix products, arithmetic and copies ran while one was open for 4% -> 3% of each run, Pallas kernels for 0% -> 0%
where the time goes in v1:
time: 92.8 us; the launch traced here: 92 us
  starting transfers between devices  23.5 us (25%)
  Pallas kernels  18.5 us (20%)
  blocking collectives  14.9 us (16%)
  waiting for transfers between devices  14.8 us (16%)
  between operations  9.75 us (11%)
  local copies, waits for them, and re-layouts  7.47 us (8%)
  other arithmetic  3.09 us (3%)
    all_to_all x1, blocking collectives, exchange(): return lax.all_to_all(copies, axes, 0, 0, tiled=True)  14.9 us
    pallas_call x1, Pallas kernels, update(): pl.pallas_call(update_kernel, grid_spec=pltpu.PrefetchScalarGridSpec(num_...  13.6 us
    all_to_all x1, starting transfers between devices, shards(): lax.all_to_all(half, SPREAD, 0, 0, tiled=True)  10.3 us
    all_to_all x1, waiting for transfers between devices, shards(): lax.all_to_all(half, SPREAD, 0, 0, tiled=True)  9.88 us
    all_to_all x1, starting transfers between devices, exchange(): return lax.all_to_all(copies, axes, 0, 0, tiled=True)  5.62 us
    pallas_call x1, Pallas kernels, pick(): pl.pallas_call(pick_kernel, grid_spec=pltpu.PrefetchScalarGridSpec(num_sc...  4.84 us
    ppermute x1, starting transfers between devices, shards(): sib = lax.ppermute(own, 'c', [(0, 1), (1, 0)])  4.31 us
    unnamed x13, local copies, waits for them, and re-layouts  4.14 us
  transfers between devices with their start and end apart: 4, of which 3 were waited for; matrix products, arithmetic and copies ran while one was open for 3% of the time, Pallas kernels for 0%

profile of v1, /device:TPU:1, one launch (start us, length us, event | category | flops | bytes accessed | tf_op | source)
XLA Modules:
  0.0 92.0 jit_solution(4571942096876958051)
XLA Ops:
  0.6 1.3 %fusion.11 = (s32[1]{0:T(128)}, s32[1]{0:T(128)}) fusion(s32[2]{0:T(128)} %param.10), kind=kLoop, calls=%fused_computation.52 | loop fusion | bytes 16 | tf_op jit(solution)/shard_map/slice | solution.py:217
  2.0 0.7 compare_convert_fusion
  3.9 0.1 pad_add_fusion.info
  4.0 1.7 %copy-done = f32[147,4096]{1,0:T(8,128)S(1)} copy-done((f32[147,4096]{1,0:T(8,128)S(1)}, f32[147,4096]{1,0:T(8,128)}, u32[]{:S(2)}) %copy-start) | copy-done | bytes 2408472
  5.7 1.6 %copy-done.1 = f32[2,512,512]{2,1,0:T(8,128)S(1)} copy-done((f32[2,512,512]{2,1,0:T(8,128)S(1)}, f32[2,512,512]{2,1,0:T(8,128)}, u32[]{:S(2)}) %copy-start.1) | copy-done | bytes 2097176
  7.3 0.7 copy-done.3
  8.0 4.8 %pick.1 = (bf16[32,96,128]{2,1,0:T(8,128)(2,1)S(1)}, bf16[32,96,128]{2,1,0:T(8,128)(2,1)S(1)}) custom-call(s32[4]{0:T(128)S(1)} %pad_add_fusion.info, bf16[440,4096]{1,0:T(8,128)(2,1)} %feat.3, f32[147,4096]{1,0:T(8,128)S(1)} %copy-done, f32[2,512,512]{2,1,0:T(8,128)S(1)} %copy-done.1, s32[2,512]{1,0:T(2,128)S(1)} %copy-done.3), custom_call_target="tpu_custom_call" | custom-call | tf_op jit(solution)/shard_map/pick/pallas_call | solution.py:84
  12.8 3.2 %collective-permute-start = (bf16[32,96,128]{2,1,0:T(8,128)(2,1)S(1)}, bf16[32,96,128]{2,1,0:T(8,128)(2,1)S(1)}, u32[]{:S(2)}, u32[]{:S(2)}) collective-permute-start(bf16[32,96,128]{2,1,0:T(8,128)(2,1)S(1)} %get-tuple-element.5), channel_id=1, source_target_pairs={{0,2},{2,0},{1,3},{3,1},{4,6},{6,4},{5,7},{7,5},{8,10},{10,8},{9,1... | collective-permute-start | bytes 2359304 | tf_op jit(solution)/shard_map/ppermute | solution.py:225
  16.1 0.6 fusion.10
  16.7 1.3 %fusion.3 = pred[96]{0:T(512)(128)(4,1)S(1)} fusion(s32[]{:T(128)} %axis_index.69, s32[]{:T(128)} %bitcast.2, s32[]{:T(128)} %bitcast.1), kind=kLoop, calls=%fused_computation.41 | loop fusion | flops 288 | bytes 108 | tf_op jit(solution)/shard_map/eq | solution.py:227
  18.0 0.0 collective-permute-done
  18.0 1.0 %broadcast_select_fusion = bf16[32,96,128]{2,1,0:T(8,128)(2,1)} fusion(bf16[32,96,128]{2,1,0:T(8,128)(2,1)S(1)} %get-tuple-element.4, bf16[32,96,128]{2,1,0:T(8,128)(2,1)S(1)} %collective-permute-done, pred[96]{0:T(512)(128)(4,1)S(1)} %fusion.3), kind=kLoop, calls=%fused_computation | loop fusion | flops 393216 | bytes 2359392 | tf_op jit(solution)/shard_map/jit(_where)/select_n | solution.py:228
  19.0 10.3 %all-to-all-start = ((bf16[32,96,128]{2,1,0:T(8,128)(2,1)}), bf16[32,96,128]{2,1,0:T(8,128)(2,1)S(1)}, u32[]{:S(2)}, u32[]{:S(2)}) async-start(bf16[32,96,128]{2,1,0:T(8,128)(2,1)} %broadcast_select_fusion), calls=%async_computation | async-start | bytes 1572864 | tf_op jit(solution)/shard_map/all_to_all | solution.py:229
  29.3 0.7 fusion.8
  33.8 9.9 %all-to-all-done = bf16[32,96,128]{2,1,0:T(8,128)(2,1)S(1)} async-done(((bf16[32,96,128]{2,1,0:T(8,128)(2,1)}), bf16[32,96,128]{2,1,0:T(8,128)(2,1)S(1)}, u32[]{:S(2)}, u32[]{:S(2)}) %all-to-all-start) | async-done | bytes 786464 | tf_op jit(solution)/shard_map/all_to_all | solution.py:229
  43.6 0.7 broadcast_in_dim.22
  44.3 5.6 %all-to-all-start.1 = ((bf16[4,96,128]{2,1,0:T(8,128)(2,1)}), bf16[4,96,128]{2,1,0:T(8,128)(2,1)S(1)}, u32[]{:S(2)}, u32[]{:S(2)}) async-start(bf16[4,96,128]{2,1,0:T(8,128)(2,1)} %broadcast_in_dim.22), calls=%async_computation.1 | async-start | bytes 196608 | tf_op jit(solution)/shard_map/all_to_all | solution.py:211
  53.9 3.1 %all-to-all-done.1 = bf16[4,96,128]{2,1,0:T(8,128)(2,1)S(1)} async-done(((bf16[4,96,128]{2,1,0:T(8,128)(2,1)}), bf16[4,96,128]{2,1,0:T(8,128)(2,1)S(1)}, u32[]{:S(2)}, u32[]{:S(2)}) %all-to-all-start.1) | async-done | bytes 98336 | tf_op jit(solution)/shard_map/all_to_all | solution.py:211
  57.0 0.1 broadcast_in_dim.23
  57.1 14.9 %all_to_all.15.own = bf16[32,96,128]{2,1,0:T(8,128)(2,1)S(1)} all-to-all(bf16[32,96,128]{2,1,0:T(8,128)(2,1)S(1)} %broadcast_in_dim.23), channel_id=1, replica_groups=mesh['yl'=2,'zh'=4,'zl'=2,'x'=4,'c'=2,'yh'=2] {'yl','zl','x','yh'}, dimensions={0} | all-to-all | bytes 1572864 | tf_op jit(solution)/shard_map/all_to_all | solution.py:211
  72.0 4.3 %collective-permute-start.1 = (bf16[32,96,128]{2,1,0:T(8,128)(2,1)S(1)}, bf16[32,96,128]{2,1,0:T(8,128)(2,1)}, u32[]{:S(2)}, u32[]{:S(2)}) collective-permute-start(bf16[32,96,128]{2,1,0:T(8,128)(2,1)S(1)} %all_to_all.15.own), channel_id=1, source_target_pairs={{0,2},{2,0},{1,3},{3,1},{4,6},{6,4},{5,7},{7,5},{8,10},{10,8},{9,1... | collective-permute-start | bytes 2359304 | tf_op jit(solution)/shard_map/ppermute | solution.py:232
  76.3 0.1 copy.8
  76.5 1.9 %collective-permute-done.1.sib = bf16[32,96,128]{2,1,0:T(8,128)(2,1)} collective-permute-done((bf16[32,96,128]{2,1,0:T(8,128)(2,1)S(1)}, bf16[32,96,128]{2,1,0:T(8,128)(2,1)}, u32[]{:S(2)}, u32[]{:S(2)}) %collective-permute-start.1) | collective-permute-done | bytes 786464 | tf_op jit(solution)/shard_map/ppermute | solution.py:232
  78.4 13.6 %update.1 = (f32[147,4096]{1,0:T(8,128)}, f32[147,4096]{1,0:T(8,128)}) custom-call(s32[4]{0:T(128)S(1)} %pad_add_fusion.info, bf16[32,96,128]{2,1,0:T(8,128)(2,1)S(1)} %all_to_all.15.own, bf16[32,96,128]{2,1,0:T(8,128)(2,1)} %collective-permute-done.1.sib, bf16[440,4096]{1,0:T(8,128)(2,1)} %feat.3, f32[147,4096]{1,0:T(8,128)} %res.3, f32[147,4096]{1,0:T(8,128)} %coef.1, ...), custom_call_target="tpu_custom_call" | custom-call | tf_op jit(solution)/shard_map/update/pallas_call | solution.py:170
  (14 shorter events, 0.1 us)
Async XLA Ops:
  4.0 1.7 %copy-start = (f32[147,4096]{1,0:T(8,128)S(1)}, f32[147,4096]{1,0:T(8,128)}, u32[]{:S(2)}) copy-start(f32[147,4096]{1,0:T(8,128)} %res.3) | copy-start | bytes 7225348
  5.7 1.6 %copy-start.1 = (f32[2,512,512]{2,1,0:T(8,128)S(1)}, f32[2,512,512]{2,1,0:T(8,128)}, u32[]{:S(2)}) copy-start(f32[2,512,512]{2,1,0:T(8,128)} %inv.3) | copy-start | bytes 6291460
  7.3 0.7 copy-start.3
  8.0 8.1 %copy-start.5 = (s32[2]{0:T(128)S(1)}, s32[2]{0:T(128)}, u32[]{:S(2)}) copy-start(s32[2]{0:T(128)} %param.10) | copy-start | bytes 28
  12.8 5.2 %collective-permute-start = (bf16[32,96,128]{2,1,0:T(8,128)(2,1)S(1)}, bf16[32,96,128]{2,1,0:T(8,128)(2,1)S(1)}, u32[]{:S(2)}, u32[]{:S(2)}) collective-permute-start(bf16[32,96,128]{2,1,0:T(8,128)(2,1)S(1)} %get-tuple-element.5), channel_id=1, source_target_pairs={{0,2},{2,0},{1,3},{3,1},{4,6},{6,4},{5,7},{7,5},{8,10},{10,8},{9,1... | collective-permute-start | bytes 2359304 | tf_op jit(solution)/shard_map/ppermute | solution.py:225
  19.0 57.3 %copy-start.4 = (s32[2,512]{1,0:T(2,128)S(1)}, s32[2,512]{1,0:T(2,128)}, u32[]{:S(2)}) copy-start(s32[2,512]{1,0:T(2,128)} %offs.3) | copy-start | bytes 12292
  19.0 59.4 %copy-start.2 = (f32[2,512,512]{2,1,0:T(8,128)S(1)}, f32[2,512,512]{2,1,0:T(8,128)}, u32[]{:S(2)}) copy-start(f32[2,512,512]{2,1,0:T(8,128)} %inv.3) | copy-start | bytes 6291460
  19.0 24.6 %all-to-all-start = ((bf16[32,96,128]{2,1,0:T(8,128)(2,1)}), bf16[32,96,128]{2,1,0:T(8,128)(2,1)S(1)}, u32[]{:S(2)}, u32[]{:S(2)}) async-start(bf16[32,96,128]{2,1,0:T(8,128)(2,1)} %broadcast_select_fusion), calls=%async_computation | async-start | bytes 1572864 | tf_op jit(solution)/shard_map/all_to_all | solution.py:229
  44.3 12.7 %all-to-all-start.1 = ((bf16[4,96,128]{2,1,0:T(8,128)(2,1)}), bf16[4,96,128]{2,1,0:T(8,128)(2,1)S(1)}, u32[]{:S(2)}, u32[]{:S(2)}) async-start(bf16[4,96,128]{2,1,0:T(8,128)(2,1)} %broadcast_in_dim.22), calls=%async_computation.1 | async-start | bytes 196608 | tf_op jit(solution)/shard_map/all_to_all | solution.py:211
  72.0 6.4 %collective-permute-start.1 = (bf16[32,96,128]{2,1,0:T(8,128)(2,1)S(1)}, bf16[32,96,128]{2,1,0:T(8,128)(2,1)}, u32[]{:S(2)}, u32[]{:S(2)}) collective-permute-start(bf16[32,96,128]{2,1,0:T(8,128)(2,1)S(1)} %all_to_all.15.own), channel_id=1, source_target_pairs={{0,2},{2,0},{1,3},{3,1},{4,6},{6,4},{5,7},{7,5},{8,10},{10,8},{9,1... | collective-permute-start | bytes 2359304 | tf_op jit(solution)/shard_map/ppermute | solution.py:232
